TPU v7x, 32 devices: a whole 2x2x4 slice. The times are simulated.
32 devices in a mesh: net: 4 (over z), seg: 2 (over y), corner: 4 (over x, core).
Axes of the slice: x: 2, y: 2, z: 4, core: 2. Of those that a mesh axis runs over, the one named last changes fastest.
Arguments:
- tile_values: bfloat16 [512, 128, 1024], P(('net', 'seg', 'corner')), may hold values from -48 to 48
- tile_coords: int32 [512, 3], P(('net', 'seg', 'corner')), may hold values from 0 to 31, as said below
- tile_count: int32 [32], P(('net', 'seg', 'corner')), may hold values from 12 to 16, as said below
- owner_map: int32 [32], P('net'), may hold values from 0 to 31, as said below
- corner_factor: bfloat16 [64, 256], P('corner')
- seg_factor: bfloat16 [4096, 256], P(('seg', 'net'))
Outputs:
- net_factor: float32 [4096, 256], P(('net', 'seg', 'corner'))
Inputs may be any that keep to these rules, and one draw needn't show every extreme that they name: `tile_coords`: row t of device d gives a corner block within the corner range stored by d's corner index, a net block that owner_map assigns to an owner slot of d's net index, and a segment block within the segment range of d's seg index. Among a device's 16 rows at most 4 name segment blocks stored by any one device of the net axis, and on every device two live rows name segment blocks stored by the same device of the net axis. The first tile_count[d] rows of device d are live; the others are ignored. `owner_map`: A permutation of the 32 net blocks.
All inputs are finite; a program needn't handle non-finite values.
Results may differ from a plain program's by a relative error of at most 0.0058.
The roundings to bfloat16 on the way count: a program that leaves them out, or rounds other values in their place, can miss the bound.
Values may be sent and summed in bfloat16 or wider, within the bound.
A program may use at most 64 MiB of HBM per device.

v0:
```python
import functools

import jax
import jax.numpy as jnp
from jax import lax
from jax.experimental import pallas as pl
from jax.experimental.pallas import tpu as pltpu
from jax.sharding import PartitionSpec as P

CBLK = 8
MESH = pl.DeviceIdType.MESH
HIGH = lax.Precision.HIGHEST
PAIR = 2


def dot32(a, b, dims=((1,), (0,))):
    return lax.dot_general(a, b, (dims, ((), ())), precision=HIGH, preferred_element_type=jnp.float32)


def invert(s):
    n = s.shape[0]
    row = lax.broadcasted_iota(jnp.int32, (n, n), 0)
    col = lax.broadcasted_iota(jnp.int32, (n, n), 1)
    sub, lane = row[:8], col[:8]
    s = s.reshape(n // 8, 8, n)
    for k in range(0, n, 4):
        g, o = divmod(k, 8)
        cols = [jnp.broadcast_to(s[:, :, k + j : k + j + 1], s.shape) for j in range(4)]
        own = s[g]
        block = {
            (i, j): jnp.broadcast_to(cols[j][g][o + i : o + i + 1, :], (8, n))
            for i in range(4)
            for j in range(i, 4)
        }
        rows = [
            jnp.broadcast_to(own[o + i : o + i + 1, :], (8, n)) - jnp.where(lane == k + i, 1.0, 0.0)
            for i in range(4)
        ]
        scale = 1.0 / (block[0, 0] * block[1, 1] - block[0, 1] * block[0, 1])
        p00, p01, p11 = block[1, 1] * scale, -block[0, 1] * scale, block[0, 0] * scale
        v02 = p00 * block[0, 2] + p01 * block[1, 2]
        v03 = p00 * block[0, 3] + p01 * block[1, 3]
        v12 = p01 * block[0, 2] + p11 * block[1, 2]
        v13 = p01 * block[0, 3] + p11 * block[1, 3]
        c22 = block[2, 2] - (block[0, 2] * v02 + block[1, 2] * v12)
        c23 = block[2, 3] - (block[0, 2] * v03 + block[1, 2] * v13)
        c33 = block[3, 3] - (block[0, 3] * v03 + block[1, 3] * v13)
        scale = 1.0 / (c22 * c33 - c23 * c23)
        w0 = p00 * rows[0] + p01 * rows[1]
        w1 = p01 * rows[0] + p11 * rows[1]
        t2 = (rows[2] - (v02 * rows[0] + v12 * rows[1])) * scale
        t3 = (rows[3] - (v03 * rows[0] + v13 * rows[1])) * scale
        u2 = c33 * t2 - c23 * t3
        u3 = c22 * t3 - c23 * t2
        u0 = w0 - (v02 * u2 + v03 * u3)
        u1 = w1 - (v12 * u2 + v13 * u3)
        add = sum(jnp.where(sub == o + j, u, 0.0) for j, u in enumerate((u0, u1, u2, u3)))
        s = s - ((cols[0] * u0 + cols[1] * u1) + (cols[2] * u2 + cols[3] * u3))
        parts = [s[:g], (s[g] + add)[None], s[g + 1 :]]
        s = jnp.concatenate([part for part in parts if part.shape[0]], axis=0)
    return jnp.where(row == col, 2.0, 0.0) - s.reshape(n, n)


def kernel(
    nn, ns, nc, coords_ref, count_ref, owner_ref, corner_hbm, seg_ref, values_ref, out_ref,
    coords, count, owner, corner_ref,
    gathered, corner_all, corner_wide, values, partial, gram_in, gram_own, gram_all,
    summed, pair_in, rows_in, square, upper, local_sem, small_sem, z_send, z_recv, c_send, c_recv,
    h_send, h_recv, l_send, l_recv, g_send, g_recv, p_send, p_recv, s_send, s_recv,
):
    net, seg, corner = lax.axis_index("net"), lax.axis_index("seg"), lax.axis_index("corner")
    highs = nc // PAIR
    high, low = corner // PAIR, lax.rem(corner, PAIR)
    other_low = high * PAIR + 1 - low
    group = ns * nc
    pairs = group // PAIR
    slot = seg * nc + corner
    mine = seg * highs + high
    slots = values.shape[0]
    columns = corner_ref.shape[1]
    half = columns // 2
    held = gathered.shape[0] // nn
    chunk = held // nc
    net_rows = values.shape[1]

    def remote(src, dst, send, recv, **where):
        return pltpu.make_async_remote_copy(
            src_ref=src, dst_ref=dst, send_sem=send, recv_sem=recv, device_id=where, device_id_type=MESH
        )

    parts = local_sem.shape[0] - 1
    step = slots // parts
    loads = [
        pltpu.make_async_copy(
            values_ref.at[pl.ds(i * step, step)], values.at[pl.ds(i * step, step)], local_sem.at[i]
        )
        for i in range(parts)
    ]
    own_seg = pltpu.make_async_copy(seg_ref, gathered.at[pl.ds(net * held, held)], local_sem.at[parts])
    small = [
        pltpu.make_async_copy(source, to, small_sem.at[i])
        for i, (source, to) in enumerate(
            ((corner_hbm, corner_ref), (coords_ref, coords), (count_ref, count), (owner_ref, owner))
        )
    ]
    for copy in small:
        copy.start()
    own_seg.start()
    for load in loads:
        load.start()

    small[0].wait()
    barrier = pltpu.get_barrier_semaphore()
    for i in range(1, group):
        peer = lax.rem(slot + i, group)
        pl.semaphore_signal(
            barrier, inc=1, device_id={"seg": peer // nc, "corner": lax.rem(peer, nc)}, device_id_type=MESH
        )
    for i in range(1, nn):
        pl.semaphore_signal(barrier, inc=1, device_id={"net": lax.rem(net + i, nn)}, device_id_type=MESH)
    pl.semaphore_wait(barrier, group + nn - 2)

    def block(source, which):
        return pl.ds(source * held + which * chunk, chunk)

    sends = []

    def go(copy):
        copy.start()
        sends.append(copy)

    for i in range(1, nn):
        go(
            remote(
                seg_ref.at[pl.ds(corner * chunk, chunk)], gathered.at[block(net, corner)],
                z_send.at[i - 1], z_recv.at[i - 1], net=lax.rem(net + i, nn),
            )
        )
    for i in range(1, nc):
        go(
            remote(
                corner_ref, corner_all.at[corner], c_send.at[i - 1], c_recv.at[i - 1],
                corner=lax.rem(corner + i, nc),
            )
        )
    corner_all[pl.ds(corner, 1)] = corner_ref[...][None]
    corner_wide[...] = corner_ref[...].astype(jnp.float32).reshape(corner_wide.shape)

    def gram_of(source):
        rows = gathered[pl.ds(source * held, held)].reshape(-1, columns)
        left = gathered[pl.ds(source * held, held), :, pl.ds(pl.multiple_of(low * half, half), half)]
        return lax.dot_general(
            left.reshape(-1, half), rows, (((0,), (0,)), ((), ())), preferred_element_type=jnp.float32
        )

    own_seg.wait()
    gram_own[...] = gram_of(net)

    for i in range(1, nn):
        source = lax.rem(net - i + nn, nn)
        got = gathered.at[block(source, corner)]
        remote(got, got, z_send.at[i - 1], z_recv.at[i - 1], net=source).wait_recv()
        for j in range(1, highs):
            at = (i - 1) * (highs - 1) + j - 1
            go(
                remote(
                    got, got, h_send.at[at], h_recv.at[at], corner=lax.rem(high + j, highs) * PAIR + low
                )
            )
        at = (i - 1) * highs
        go(remote(got, got, l_send.at[at], l_recv.at[at], corner=other_low))
    for i in range(1, nn):
        source = lax.rem(net - i + nn, nn)
        for j in range(1, highs):
            at = (i - 1) * (highs - 1) + j - 1
            got = gathered.at[block(source, lax.rem(high - j + highs, highs) * PAIR + low)]
            remote(got, got, h_send.at[at], h_recv.at[at], corner=other_low).wait_recv()
            to = (i - 1) * highs + j
            go(remote(got, got, l_send.at[to], l_recv.at[to], corner=other_low))
    for i in range(1, nn):
        source = lax.rem(net - i + nn, nn)
        for j in range(highs):
            at = (i - 1) * highs + j
            got = gathered.at[block(source, lax.rem(high - j + highs, highs) * PAIR + 1 - low)]
            remote(got, got, l_send.at[at], l_recv.at[at], corner=other_low).wait_recv()
        gram_own[...] += gram_of(source)

    for j in range(1, ns):
        go(
            remote(
                gram_own, gram_in.at[j - 1], g_send.at[j - 1], g_recv.at[j - 1], seg=lax.rem(seg + j, ns)
            )
        )
    for load in loads + small[1:]:
        load.wait()

    corner_span, seg_span = corner_ref.shape[0] // CBLK, held * nn

    def tile(t, carry):
        corner_rows = corner_wide[lax.rem(coords[0, t], corner_span)]
        seg_rows = gathered[lax.rem(coords[2, t], seg_span)].astype(jnp.float32)
        khatri = jnp.concatenate(
            [(corner_rows[a : a + 1, :] * seg_rows).astype(jnp.bfloat16) for a in range(CBLK)], axis=0
        )
        partial[t] = jnp.dot(values[t], khatri, preferred_element_type=jnp.float32)
        return carry

    lax.fori_loop(0, slots // 2, tile, 0)

    total = gram_own[...]
    for j in range(1, ns):
        remote(
            gram_own, gram_in.at[j - 1], g_send.at[j - 1], g_recv.at[j - 1], seg=lax.rem(seg + j, ns)
        ).wait_recv()
        total = total + gram_in[j - 1]
    gram_all[pl.ds(low, 1)] = total[None]
    go(
        remote(
            gram_all.at[low], gram_all.at[low], g_send.at[ns - 1], g_recv.at[ns - 1], corner=other_low
        )
    )

    lax.fori_loop(slots // 2, slots, tile, 0)

    live = count[0]

    def add_up(q):
        block_of = owner[q]
        acc = jnp.zeros((net_rows, columns), jnp.float32)
        for t in range(slots):
            take = jnp.logical_and(coords[1, t] == block_of, t < live)
            acc = acc + jnp.where(take, partial[t], 0.0)
        return acc

    def pair_copy(h):
        return remote(
            summed.at[h * PAIR + 1 - low], pair_in.at[h], p_send.at[h], p_recv.at[h], corner=other_low
        )

    def give(h, carry):
        summed[pl.ds(h * PAIR + 1 - low, 1)] = add_up(h * PAIR + 1 - low)[None]
        pair_copy(h).start()
        return carry

    def keep(h, carry):
        summed[pl.ds(h * PAIR + low, 1)] = add_up(h * PAIR + low)[None]
        return carry

    lax.fori_loop(0, pairs, give, 0)
    lax.fori_loop(0, pairs, keep, 0)

    def row_copy(i):
        h = lax.rem(mine + i, pairs)
        return remote(
            summed.at[h * PAIR + low], rows_in.at[i - 1], s_send.at[i - 1], s_recv.at[i - 1],
            seg=h // highs, corner=lax.rem(h, highs) * PAIR + low,
        )

    def pass_on(i, carry):
        h = lax.rem(mine + i, pairs)
        got = pair_in.at[h]
        remote(got, got, p_send.at[h], p_recv.at[h], corner=other_low).wait_recv()
        at = h * PAIR + low
        summed[pl.ds(at, 1)] = summed[pl.ds(at, 1)] + pair_in[pl.ds(h, 1)]

        @pl.when(i < pairs)
        def _():
            row_copy(i).start()

        return carry

    lax.fori_loop(1, pairs + 1, pass_on, 0)

    for i in range(1, nc):
        remote(
            corner_ref, corner_all.at[lax.rem(corner - i + nc, nc)], c_send.at[i - 1], c_recv.at[i - 1],
            corner=lax.rem(corner + i, nc),
        ).wait_recv()
    remote(
        gram_all.at[low], gram_all.at[1 - low], g_send.at[ns - 1], g_recv.at[ns - 1], corner=other_low
    ).wait_recv()
    factor = corner_all[...].reshape(-1, columns)
    gram = lax.dot_general(factor, factor, (((0,), (0,)), ((), ())), preferred_element_type=jnp.float32)
    gram = gram * gram_all[...].reshape(columns, columns)
    row = lax.broadcasted_iota(jnp.int32, (columns, 1), 0)
    col = lax.broadcasted_iota(jnp.int32, (1, columns), 1)
    diag = jnp.where(row == col, gram, 0.0)
    scale_row = lax.rsqrt(jnp.sum(diag, axis=0, keepdims=True))
    scale_col = lax.rsqrt(jnp.sum(diag, axis=1, keepdims=True))
    gram = gram * scale_col * scale_row
    square[0] = gram[:half, :half]
    square[1] = gram[half:, half:]
    upper[0] = gram[:half, half:]

    def halves(h, carry):
        square[h] = invert(square[h])

        @pl.when(h == 0)
        def _():
            upper[1] = dot32(square[0], upper[0])
            square[1] = square[1] - dot32(upper[0], upper[1], ((0,), (0,)))

        return carry

    lax.fori_loop(0, 2, halves, 0)

    def take_rows(i, acc):
        row_copy(i).wait_recv()
        return acc + rows_in[i - 1]

    mttkrp = lax.fori_loop(1, pairs, take_rows, summed[slot]) * scale_row
    first, second = mttkrp[:, :half], mttkrp[:, half:]
    second = dot32(second - dot32(first, upper[1]), square[1])
    first = dot32(first - dot32(second, upper[0], ((1,), (1,))), square[0])
    out_ref[:, :half] = first * scale_row[:, :half]
    out_ref[:, half:] = second * scale_row[:, half:]

    for copy in sends:
        copy.wait_send()

    def end_pair(h, carry):
        pair_copy(h).wait_send()
        return carry

    def end_row(i, carry):
        row_copy(i).wait_send()
        return carry

    lax.fori_loop(0, pairs, end_pair, 0)
    lax.fori_loop(1, pairs, end_row, 0)


def body(tile_values, tile_coords, tile_count, owner_map, corner_factor, seg_factor):
    nn, ns, nc = lax.axis_size("net"), lax.axis_size("seg"), lax.axis_size("corner")
    slots, net_rows, depth = tile_values.shape
    columns = corner_factor.shape[1]
    width = depth // CBLK
    held = seg_factor.shape[0] // width
    group = ns * nc
    pairs, highs, half = group // PAIR, nc // PAIR, columns // 2
    vmem = pl.BlockSpec(memory_space=pltpu.VMEM)
    hbm = pl.BlockSpec(memory_space=pltpu.HBM)
    dma = lambda n: pltpu.SemaphoreType.DMA((max(n, 1),))
    f32, bf16 = jnp.float32, jnp.bfloat16
    return pl.pallas_call(
        functools.partial(kernel, nn, ns, nc),
        out_shape=jax.ShapeDtypeStruct((net_rows, columns), f32),
        in_specs=[hbm] * 6,
        out_specs=vmem,
        scratch_shapes=[
            pltpu.SMEM((3, slots), jnp.int32),
            pltpu.SMEM(tile_count.shape, jnp.int32),
            pltpu.SMEM(owner_map.shape, jnp.int32),
            pltpu.VMEM(corner_factor.shape, bf16),
            pltpu.VMEM((nn * held, width, columns), bf16),
            pltpu.VMEM((nc,) + corner_factor.shape, bf16),
            pltpu.VMEM((corner_factor.shape[0] // CBLK, CBLK, columns), f32),
            pltpu.VMEM(tile_values.shape, bf16),
            pltpu.VMEM((slots, net_rows, columns), f32),
            pltpu.VMEM((max(ns - 1, 1), half, columns), f32),
            pltpu.VMEM((half, columns), f32),
            pltpu.VMEM((2, half, columns), f32),
            pltpu.VMEM((group, net_rows, columns), f32),
            pltpu.VMEM((pairs, net_rows, columns), f32),
            pltpu.VMEM((max(pairs - 1, 1), net_rows, columns), f32),
            pltpu.VMEM((2, half, half), f32),
            pltpu.VMEM((2, half, half), f32),
            dma(5), dma(4),
            dma(nn - 1), dma(nn - 1), dma(nc - 1), dma(nc - 1),
            dma((nn - 1) * (highs - 1)), dma((nn - 1) * (highs - 1)),
            dma((nn - 1) * highs), dma((nn - 1) * highs),
            dma(ns), dma(ns), dma(pairs), dma(pairs), dma(pairs - 1), dma(pairs - 1),
        ],
        compiler_params=pltpu.CompilerParams(
            collective_id=0, has_side_effects=True, vmem_limit_bytes=63 * 1024 * 1024
        ),
    )(
        tile_coords.T, tile_count, owner_map, corner_factor,
        seg_factor.reshape(held, width, columns), tile_values,
    )


def solution(mesh):
    return jax.shard_map(
        body,
        mesh=mesh,
        in_specs=(
            P(("net", "seg", "corner"), None, None),
            P(("net", "seg", "corner"), None),
            P(("net", "seg", "corner")),
            P("net"),
            P("corner", None),
            P(("seg", "net"), None),
        ),
        out_specs=P(("net", "seg", "corner"), None),
        check_vma=False,
    )
```

profile of v0, /device:TPU:0, one launch (start us, length us, event | category | flops | bytes accessed | tf_op | source)
XLA Modules:
  0.0 41.7 jit_solution(5299165228036215937)
XLA Ops:
  0.7 39.5 %shard_map.64 = f32[128,256]{1,0:T(8,128)} custom-call(s32[3,16]{1,0:T(4,128)} %bitcast.3, s32[1]{0:T(128)S(6)} %copy.8.count_ref, s32[8]{0:T(128)} %owner_ref.1, bf16[16,256]{1,0:T(8,128)(2,1)} %corner_hbm.1, bf16[4,128,256]{2,1,0:T(8,128)(2,1)} %bitcast.2, bf16[16,128,1024]{2,1,0:T(8,128)(2,1)} %values_ref.1), custom_call_target="tpu_custom_call" | custom-call | tf_op jit(solution)/shard_map/pallas_call | solution.py:345
  40.1 1.6 %copy.9 = f32[128,256]{1,0:T(8,128)} copy(f32[128,256]{1,0:T(8,128)} %shard_map.64) | data formatting | bytes 262144
where the time goes:
time: 41.9 us; the launch traced here: 41.7 us
  Pallas kernels  39.5 us (94%)
  local copies, waits for them, and re-layouts  1.57 us (4%)
  between operations  0.66 us (2%)
    pallas_call x1, Pallas kernels, body(): pl.pallas_call(functools.partial(kernel, nn, ns, nc), out_shape=jax.Shape...  39.5 us
    unnamed x1, local copies, waits for them, and re-layouts  1.57 us

commit v1 on v0

--- a/solution.py
+++ b/solution.py
@@ -62,7 +62,7 @@
 
 
 def kernel(
-    nn, ns, nc, coords_ref, count_ref, owner_ref, corner_hbm, seg_ref, values_ref, out_ref,
+    nn, ns, nc, coords_ref, count_ref, owner_ref, corner_hbm, seg_ref, values_ref, out_ref, scale_ref,
     coords, count, owner, corner_ref,
     gathered, corner_all, corner_wide, values, partial, gram_in, gram_own, gram_all,
     summed, pair_in, rows_in, square, upper, local_sem, small_sem, z_send, z_recv, c_send, c_recv,
@@ -196,16 +196,20 @@
 
     corner_span, seg_span = corner_ref.shape[0] // CBLK, held * nn
 
-    def tile(t, carry):
+    def tile(t):
         corner_rows = corner_wide[lax.rem(coords[0, t], corner_span)]
         seg_rows = gathered[lax.rem(coords[2, t], seg_span)].astype(jnp.float32)
         khatri = jnp.concatenate(
             [(corner_rows[a : a + 1, :] * seg_rows).astype(jnp.bfloat16) for a in range(CBLK)], axis=0
         )
         partial[t] = jnp.dot(values[t], khatri, preferred_element_type=jnp.float32)
-        return carry
-
-    lax.fori_loop(0, slots // 2, tile, 0)
+
+    def four_tiles(i, carry):
+        for j in range(4):
+            tile(i * 4 + j)
+        return carry
+
+    lax.fori_loop(0, slots // 8, four_tiles, 0)
 
     total = gram_own[...]
     for j in range(1, ns):
@@ -220,7 +224,7 @@
         )
     )
 
-    lax.fori_loop(slots // 2, slots, tile, 0)
+    lax.fori_loop(slots // 8, slots // 4, four_tiles, 0)
 
     live = count[0]
 
@@ -312,8 +316,9 @@
     first, second = mttkrp[:, :half], mttkrp[:, half:]
     second = dot32(second - dot32(first, upper[1]), square[1])
     first = dot32(first - dot32(second, upper[0], ((1,), (1,))), square[0])
-    out_ref[:, :half] = first * scale_row[:, :half]
-    out_ref[:, half:] = second * scale_row[:, half:]
+    out_ref[:, :half] = first
+    out_ref[:, half:] = second
+    scale_ref[...] = jnp.broadcast_to(scale_row, scale_ref.shape)
 
     for copy in sends:
         copy.wait_send()
@@ -342,11 +347,11 @@
     hbm = pl.BlockSpec(memory_space=pltpu.HBM)
     dma = lambda n: pltpu.SemaphoreType.DMA((max(n, 1),))
     f32, bf16 = jnp.float32, jnp.bfloat16
-    return pl.pallas_call(
+    rows, scale = pl.pallas_call(
         functools.partial(kernel, nn, ns, nc),
-        out_shape=jax.ShapeDtypeStruct((net_rows, columns), f32),
+        out_shape=(jax.ShapeDtypeStruct((net_rows, columns), f32), jax.ShapeDtypeStruct((8, columns), f32)),
         in_specs=[hbm] * 6,
-        out_specs=vmem,
+        out_specs=(vmem, vmem),
         scratch_shapes=[
             pltpu.SMEM((3, slots), jnp.int32),
             pltpu.SMEM(tile_count.shape, jnp.int32),
@@ -378,6 +383,7 @@
         tile_coords.T, tile_count, owner_map, corner_factor,
         seg_factor.reshape(held, width, columns), tile_values,
     )
+    return (rows.reshape(-1, *scale.shape) * scale).reshape(rows.shape)
 
 
 def solution(mesh):

time: 41.9 us -> 40.9 us (0.976)
  other arithmetic: 0 us -> 1.57 us
  local copies, waits for them, and re-layouts: 1.57 us -> 0 us
  Pallas kernels: 39.5 us -> 38.5 us
    mul x0 -> x1, other arithmetic: none -> 1.57 us  [body(): return (rows.reshape(-1, *scale.shape) * scale).reshape(rows.shape)]
    unnamed x1 -> x0, local copies, waits for them, and re-layouts: 1.57 us -> none
    pallas_call x1, Pallas kernels: 39.5 us -> 38.5 us  [body(): pl.pallas_call(functools.partial(kernel, nn, ns, nc), out_shape=(jax.Shap...]
where the time goes in v1:
time: 40.9 us; the launch traced here: 40.7 us
  Pallas kernels  38.5 us (94%)
  other arithmetic  1.57 us (4%)
  between operations  0.66 us (2%)
    pallas_call x1, Pallas kernels, body(): pl.pallas_call(functools.partial(kernel, nn, ns, nc), out_shape=(jax.Shap...  38.5 us
    mul x1, other arithmetic, body(): return (rows.reshape(-1, *scale.shape) * scale).reshape(rows.shape)  1.57 us

profile of v1, /device:TPU:0, one launch (start us, length us, event | category | flops | bytes accessed | tf_op | source)
XLA Modules:
  0.0 40.7 jit_solution(18215914015615681127)
XLA Ops:
  0.7 38.5 %shard_map.64 = (f32[128,256]{1,0:T(8,128)}, f32[8,256]{1,0:T(8,128)}) custom-call(s32[3,16]{1,0:T(4,128)} %bitcast.5, s32[1]{0:T(128)S(6)} %copy.7.count_ref, s32[8]{0:T(128)} %owner_ref.1, bf16[16,256]{1,0:T(8,128)(2,1)} %corner_hbm.1, bf16[4,128,256]{2,1,0:T(8,128)(2,1)} %bitcast.4, bf16[16,128,1024]{2,1,0:T(8,128)(2,1)} %values_ref.1), custom_call_target="tpu_custom_call" | custom-call | tf_op jit(solution)/shard_map/pallas_call | solution.py:350
  39.1 1.6 %bitcast_multiply_fusion = f32[128,256]{1,0:T(8,128)} fusion(f32[128,256]{1,0:T(8,128)} %get-tuple-element.7, f32[8,256]{1,0:T(8,128)} %get-tuple-element.8), kind=kLoop, calls=%fused_computation | loop fusion | flops 32768 | bytes 270336 | tf_op jit(solution)/shard_map/mul | solution.py:386

commit v2 on v1

--- a/solution.py
+++ b/solution.py
@@ -197,10 +197,10 @@
     corner_span, seg_span = corner_ref.shape[0] // CBLK, held * nn
 
     def tile(t):
-        corner_rows = corner_wide[lax.rem(coords[0, t], corner_span)]
-        seg_rows = gathered[lax.rem(coords[2, t], seg_span)].astype(jnp.float32)
+        corner_rows = corner_wide[lax.rem(coords[0, t], corner_span)].astype(jnp.bfloat16)
+        seg_rows = gathered[lax.rem(coords[2, t], seg_span)]
         khatri = jnp.concatenate(
-            [(corner_rows[a : a + 1, :] * seg_rows).astype(jnp.bfloat16) for a in range(CBLK)], axis=0
+            [corner_rows[a : a + 1, :] * seg_rows for a in range(CBLK)], axis=0
         )
         partial[t] = jnp.dot(values[t], khatri, preferred_element_type=jnp.float32)
 

time: 40.9 us -> 40.8 us (level)
  no operation moved by 1% of the time
where the time goes in v2:
time: 40.8 us; the launch traced here: 40.6 us
  Pallas kernels  38.4 us (94%)
  other arithmetic  1.57 us (4%)
  between operations  0.66 us (2%)
    pallas_call x1, Pallas kernels, body(): pl.pallas_call(functools.partial(kernel, nn, ns, nc), out_shape=(jax.Shap...  38.4 us
    mul x1, other arithmetic, body(): return (rows.reshape(-1, *scale.shape) * scale).reshape(rows.shape)  1.57 us

profile of v2, /device:TPU:0, one launch (start us, length us, event | category | flops | bytes accessed | tf_op | source)
XLA Modules:
  0.0 40.6 jit_solution(14693556639168900519)
XLA Ops:
  0.7 38.4 %shard_map.64 = (f32[128,256]{1,0:T(8,128)}, f32[8,256]{1,0:T(8,128)}) custom-call(s32[3,16]{1,0:T(4,128)} %bitcast.5, s32[1]{0:T(128)S(6)} %copy.7.count_ref, s32[8]{0:T(128)} %owner_ref.1, bf16[16,256]{1,0:T(8,128)(2,1)} %corner_hbm.1, bf16[4,128,256]{2,1,0:T(8,128)(2,1)} %bitcast.4, bf16[16,128,1024]{2,1,0:T(8,128)(2,1)} %values_ref.1), custom_call_target="tpu_custom_call" | custom-call | tf_op jit(solution)/shard_map/pallas_call | solution.py:350
  39.0 1.6 %bitcast_multiply_fusion = f32[128,256]{1,0:T(8,128)} fusion(f32[128,256]{1,0:T(8,128)} %get-tuple-element.7, f32[8,256]{1,0:T(8,128)} %get-tuple-element.8), kind=kLoop, calls=%fused_computation | loop fusion | flops 32768 | bytes 270336 | tf_op jit(solution)/shard_map/mul | solution.py:386
